TPU v7x, 128 devices: a whole 4x4x4 slice. The times are simulated.
128 devices in a mesh: freq: 8 (over x_lo, y), tm: 16 (over z, x_hi, core).
Axes of the slice: x: 4 (x_hi: 2, x_lo: 2; x = x_hi * 2 + x_lo), y: 4, z: 4, core: 2. Of those that a mesh axis runs over, the one named last changes fastest.
Arguments:
- spectra: bfloat16 [2, 64, 2, 256, 3072], P(None, 'tm', None, None, 'freq'), may hold values from -6 to 6
- w_embed: bfloat16 [128, 1024], replicated, may hold values from -0.5 to 0.5
- w_query: bfloat16 [1, 1024, 1024], replicated, may hold values from -1 to 1
- w_key: bfloat16 [1, 1024, 1024], replicated, may hold values from -3 to 3
- w_value: bfloat16 [1, 1024, 1024], replicated, may hold values from -0.1875 to 0.1875
- w_out: bfloat16 [1, 1024, 1024], replicated, may hold values from -0.1875 to 0.1875
- norm_gains: float32 [1, 2, 1024], replicated, may hold values from 0.1 to 1.9
- w_gate: bfloat16 [1, 1024, 2048], replicated, may hold values from -0.1875 to 0.1875
- w_up: bfloat16 [1, 1024, 2048], replicated, may hold values from -0.1875 to 0.1875
- w_down: bfloat16 [1, 2048, 1024], replicated, may hold values from -0.125 to 0.125
- w_head: bfloat16 [1024, 128], replicated, may hold values from -0.1875 to 0.1875
Outputs:
- predicted: bfloat16 [2, 256, 256, 128], P(None, 'tm', 'freq')
All inputs are finite; a program needn't handle non-finite values.
Results may differ from a plain program's by a relative error of at most 0.033.
Values may be sent and summed in bfloat16 or wider, within the bound.
A program may use at most 128 MiB of HBM per device.

v0:
```python
import math

import jax
import jax.numpy as jnp
from jax import lax
from jax.sharding import PartitionSpec as P

DELAY_TAPS = 256
HEAD_DIM = 128
TILE = 32


def fourier_table(count, out_count, total):
    rows = jnp.arange(count, dtype=jnp.int32)
    cols = jnp.arange(out_count, dtype=jnp.int32)
    product = rows[:, None] * cols[None, :] % total
    angle = 2.0 * math.pi / total * product.astype(jnp.float32)
    factor = 1.0 / math.sqrt(total)
    cosine = jnp.cos(angle) * factor
    sine = jnp.sin(angle) * factor
    real_rows = jnp.stack([cosine, -sine], axis=-1)
    imag_rows = jnp.stack([sine, cosine], axis=-1)
    return jnp.stack([real_rows, imag_rows], axis=0).astype(jnp.bfloat16)


def normed(values):
    return values * lax.rsqrt(jnp.mean(values * values, axis=-1, keepdims=True) + 1e-05)


def network(
    feature_rows, w_embed, w_query, w_key, w_value, w_out, norm_gains, w_gate, w_up, w_down, w_head
):
    count = feature_rows.shape[0]
    width = w_embed.shape[1]
    heads = width // HEAD_DIM
    state = jnp.dot(feature_rows, w_embed, preferred_element_type=jnp.float32).astype(jnp.bfloat16)
    hnorm = (normed(state.astype(jnp.float32)) * norm_gains[0, 0]).astype(jnp.bfloat16)
    query = jnp.dot(hnorm, w_query[0], preferred_element_type=jnp.float32).astype(jnp.bfloat16)
    keyed = jnp.dot(hnorm, w_key[0], preferred_element_type=jnp.float32).astype(jnp.bfloat16)
    valued = jnp.dot(hnorm, w_value[0], preferred_element_type=jnp.float32).astype(jnp.bfloat16)
    shape4 = (count // TILE, TILE, heads, HEAD_DIM)
    scores = jnp.einsum(
        "bqhd,bkhd->bhqk",
        query.reshape(shape4),
        keyed.reshape(shape4),
        preferred_element_type=jnp.float32,
    ) * HEAD_DIM ** (-0.5)
    weights = jax.nn.softmax(scores, axis=-1).astype(jnp.bfloat16)
    mixed = (
        jnp.einsum(
            "bhqk,bkhd->bqhd", weights, valued.reshape(shape4), preferred_element_type=jnp.float32
        )
        .astype(jnp.bfloat16)
        .reshape(count, width)
    )
    state = (
        state.astype(jnp.float32) + jnp.dot(mixed, w_out[0], preferred_element_type=jnp.float32)
    ).astype(jnp.bfloat16)
    hnorm = (normed(state.astype(jnp.float32)) * norm_gains[0, 1]).astype(jnp.bfloat16)
    gate = jnp.dot(hnorm, w_gate[0], preferred_element_type=jnp.float32)
    upward = jnp.dot(hnorm, w_up[0], preferred_element_type=jnp.float32)
    hidden = (jax.nn.silu(gate) * upward).astype(jnp.bfloat16)
    state = (
        state.astype(jnp.float32) + jnp.dot(hidden, w_down[0], preferred_element_type=jnp.float32)
    ).astype(jnp.bfloat16)
    final = normed(state.astype(jnp.float32)).astype(jnp.bfloat16)
    return jnp.dot(final, w_head, preferred_element_type=jnp.float32).astype(jnp.bfloat16)


def body(
    spectra, w_embed, w_query, w_key, w_value, w_out, norm_gains, w_gate, w_up, w_down, w_head
):
    freq_count = lax.axis_size("freq")
    slot_groups = lax.axis_size("tm")
    users, slot_share, _, antennas, sub_share = spectra.shape
    slots = slot_share * slot_groups
    subcarriers = sub_share * freq_count
    doppler_table = fourier_table(slots, slots, slots)
    weights_all = (
        w_embed,
        w_query,
        w_key,
        w_value,
        w_out,
        norm_gains,
        w_gate,
        w_up,
        w_down,
        w_head,
    )
    blocks = spectra.reshape(users, slot_share, 2, slot_groups, antennas // slot_groups, sub_share)
    moved = lax.all_to_all(
        lax.all_to_all(blocks, "freq", split_axis=4, concat_axis=5, tiled=True),
        "tm",
        split_axis=3,
        concat_axis=1,
        tiled=True,
    )
    local = moved.reshape(users, slots, 2, -1, freq_count, sub_share)
    delay_table = fourier_table(subcarriers, DELAY_TAPS, subcarriers).reshape(
        2, freq_count, sub_share, DELAY_TAPS, 2
    )
    partial_sums = jnp.einsum(
        "uscagf,cgfte->guseat", local, delay_table, preferred_element_type=jnp.float32
    ).astype(jnp.bfloat16)
    partial_sums = lax.optimization_barrier(partial_sums)
    tap_values = jnp.sum(partial_sums.astype(jnp.float32), axis=0).astype(jnp.bfloat16)
    feature_rows = jnp.einsum(
        "usdat,dske->uatek", tap_values, doppler_table, preferred_element_type=jnp.float32
    ).astype(jnp.bfloat16)
    owned = feature_rows.shape[1]
    outcome = network(feature_rows.reshape(-1, 2 * slots), *weights_all).reshape(
        users, owned, DELAY_TAPS, 2 * slots
    )
    return lax.all_to_all(outcome, "freq", split_axis=2, concat_axis=1, tiled=True)


def solution(mesh):
    placed = (P(None, "tm", None, None, "freq"), P(), P(), P(), P(), P(), P(), P(), P(), P(), P())
    return jax.shard_map(
        body, mesh=mesh, in_specs=placed, out_specs=P(None, "tm", "freq", None), check_vma=False
    )
```

profile of v0, /device:TPU:1, one launch (start us, length us, event | category | flops | bytes accessed | tf_op | source)
XLA Modules:
  0.0 198.6 jit_solution(14206121898670590977)
XLA Ops:
  0.0 0.0 copy-start
  0.0 2.8 %copy.43 = bf16[2,4,2,16,16,384]{5,3,2,1,0,4:T(8,128)(2,1)S(1)} copy(bf16[2,4,2,16,16,384]{5,4,3,2,1,0:T(8,128)(2,1)} %bitcast.127) | data formatting | bytes 6291456 | tf_op jit(solution)/shard_map/reshape | solution.py:91
  2.8 42.8 %all_to_all.51 = bf16[2,4,2,16,16,384]{5,3,2,1,0,4:T(8,128)(2,1)S(1)} all-to-all(bf16[2,4,2,16,16,384]{5,3,2,1,0,4:T(8,128)(2,1)S(1)} %copy.43), channel_id=1, replica_groups=mesh['freq'=8,'tm'=16] {'freq'}, dimensions={4} | all-to-all | bytes 6291456 | tf_op jit(solution)/shard_map/all_to_all | solution.py:93
  45.6 3.5 %copy.44 = bf16[2,4,2,16,2,8,384]{6,5,4,2,1,0,3:T(8,128)(2,1)} copy(bf16[2,4,2,16,2,8,384]{6,3,2,1,0,4,5:T(8,128)(2,1)S(1)} %bitcast.124) | data formatting | bytes 6291456 | tf_op jit(solution)/shard_map/all_to_all | solution.py:93
  49.1 7.0 %all_to_all.40 = bf16[2,4,2,16,2,3072]{5,4,2,1,0,3:T(2,128)(2,1)} reshape(bf16[2,4,2,16,2,8,384]{6,5,4,2,1,0,3:T(8,128)(2,1)} %copy.44) | data formatting | bytes 6291456 | tf_op jit(solution)/shard_map/all_to_all | solution.py:93
  56.2 0.0 copy-start.1
  56.2 10.1 %all-to-all-start.1 = ((bf16[2,4,2,16,2,3072]{5,4,2,1,0,3:T(2,128)(2,1)}), bf16[2,4,2,16,2,3072]{5,4,2,1,0,3:T(2,128)(2,1)}, u32[]{:S(2)}, u32[]{:S(2)}) async-start(bf16[2,4,2,16,2,3072]{5,4,2,1,0,3:T(2,128)(2,1)} %all_to_all.40), calls=%async_computation.1 | async-start | bytes 6291456 | tf_op jit(solution)/shard_map/all_to_all | solution.py:92
  66.2 0.1 fusion.87
  66.4 0.2 negate_convert_fusion.1
  66.6 0.0 copy-done.1
  66.6 16.0 %negate_convert_fusion = (bf16[1,8,384,256,1]{3,2,4,1,0:T(8,128)(2,1)}, bf16[1,8,384,256,1]{3,2,4,1,0:T(8,128)(2,1)}, bf16[1,8,384,256,1]{3,2,4,1,0:T(8,128)(2,1)}) fusion(s32[8,384]{1,0:T(8,128)S(1)} %multiply_add_fusion), kind=kLoop, calls=%fused_computation.37 | loop fusion | flops 11796480 | bytes 4730880 | tf_op jit(solution)/shard_map/convert.6
  82.6 23.5 %all-to-all-done.1 = bf16[2,4,2,16,2,3072]{5,4,2,1,0,3:T(2,128)(2,1)} async-done(((bf16[2,4,2,16,2,3072]{5,4,2,1,0,3:T(2,128)(2,1)}), bf16[2,4,2,16,2,3072]{5,4,2,1,0,3:T(2,128)(2,1)}, u32[]{:S(2)}, u32[]{:S(2)}) %all-to-all-start.1) | async-done | bytes 3145760 | tf_op jit(solution)/shard_map/all_to_all | solution.py:92
  106.1 7.3 %copy.45 = bf16[2,16,4,2,1,2,3072]{6,5,3,2,1,0,4:T(2,128)(2,1)} copy(bf16[2,16,4,2,1,2,3072]{6,5,3,2,0,1,4:T(2,128)(2,1)} %bitcast.10) | data formatting | bytes 6291456 | tf_op jit(solution)/shard_map/all_to_all | solution.py:92
  113.4 8.0 %reshape.222 = bf16[2,64,2,2,8,384]{5,4,3,2,1,0:T(8,128)(2,1)} reshape(bf16[2,16,4,2,1,2,3072]{6,5,3,2,1,0,4:T(2,128)(2,1)} %copy.45) | data formatting | bytes 6291456 | tf_op jit(solution)/shard_map/reshape | solution.py:99
  121.4 6.7 %fusion.31 = bf16[8,2,64,2,2,256]{5,2,4,1,3,0:T(8,128)(2,1)} fusion(bf16[2,64,2,2,8,384,1]{5,4,3,2,1,0,6:T(8,128)(2,1)} %bitcast.128, bf16[1,8,384,256,1]{3,2,4,1,0:T(8,128)(2,1)} %get-tuple-element.9, bf16[1,8,384,256,1]{3,2,4,1,0:T(8,128)(2,1)} %get-tuple-element.8, bf16[1,8,384,256,1]{3,2,4,1,0:T(8,128)(2,1)} %get-tuple-element.7), kind=kOutput, calls=%fused_computation.46 | convolution fusion | flops 1621098496 | bytes 9961472 | tf_op jit(solution)/shard_map/uscagf,cgfte->guseat/dot_general | solution.py:103
  128.1 0.0 copy-start.5
  128.1 2.0 %reduce_sum.48 = bf16[2,64,2,2,256]{4,1,3,0,2:T(8,128)(2,1)S(1)} reduce(bf16[8,2,64,2,2,256]{5,2,4,1,3,0:T(8,128)(2,1)} %fusion.31, bf16[]{:T(256)} %constant.51.clone.1), dimensions={0}, to_apply=%region_0.1 | reduce | flops 917504 | bytes 2359298 | tf_op jit(solution)/shard_map/reduce_sum | solution.py:107
  130.2 0.3 fusion.75
  130.4 0.3 copy.50
  130.7 0.2 reshape.223
  130.9 0.0 copy-done.5
  130.9 0.8 fusion.5
  131.7 4.2 %convert_bitcast_fusion.2 = bf16[128,8,8,128]{3,1,2,0:T(8,128)(2,1)S(1)} fusion(bf16[1,1024,1024]{2,1,0:T(8,128)(2,1)} %param.13, bf16[1024,1024]{0,1:T(8,128)(2,1)S(1)} %get-tuple-element.13, f32[1024]{0:T(1024)S(1)} %bitcast.135, f32[1024]{0:T(1024)S(1)} %add_rsqrt_fusion.2), kind=kOutput, calls=%fused_computation.67 | convolution fusion | flops 2152726528 | bytes 6299648 | tf_op jit(solution)/shard_map/dot_general | solution.py:38
  135.9 0.0 copy-start.3
  135.9 0.6 copy.71
  136.5 1.0 copy-done.3
  137.5 2.6 %convert_bitcast_fusion.1 = bf16[128,8,8,128]{3,1,2,0:T(8,128)(2,1)S(1)} fusion(bf16[1,1024,1024]{2,1,0:T(8,128)(2,1)S(1)} %copy-done.3, bf16[1024,1024]{0,1:T(8,128)(2,1)S(1)} %get-tuple-element.13, f32[1024]{0:T(1024)S(1)} %bitcast.136, f32[1024]{0:T(1024)S(1)} %add_rsqrt_fusion.2), kind=kOutput, calls=%fused_computation.66 | convolution fusion | flops 2152726528 | bytes 6299648 | tf_op jit(solution)/shard_map/dot_general | solution.py:39
  140.1 0.6 copy.72
  140.7 1.2 fusion.45
  142.0 0.0 copy-start.4
  142.0 9.7 %fusion.95 = (f32[32,8,32]{2,1,0:T(8,128)S(1)}, f32[32,8,32,32]{2,3,1,0:T(8,128)S(1)}) fusion(f32[32,8,32,32]{2,3,1,0:T(8,128)S(1)} %fusion.45), kind=kOutput, calls=%fused_computation.101 | output fusion | flops 1048607 | bytes 2129920 | tf_op jit(solution)/shard_map/sub | solution.py:48
  151.7 0.0 copy-done.4
  151.7 2.7 %convert_bitcast_fusion.3 = bf16[128,8,8,128]{3,1,2,0:T(8,128)(2,1)S(1)} fusion(bf16[1,1024,1024]{2,1,0:T(8,128)(2,1)S(1)} %copy-done.4, bf16[1024,1024]{0,1:T(8,128)(2,1)S(1)} %get-tuple-element.13, f32[1024]{0:T(1024)S(1)} %bitcast.137, f32[1024]{0:T(1024)S(1)} %add_rsqrt_fusion.2), kind=kOutput, calls=%fused_computation.68 | convolution fusion | flops 2152726528 | bytes 6299648 | tf_op jit(solution)/shard_map/dot_general | solution.py:40
  154.4 0.6 copy.70
  155.0 1.0 convert_bitcast_fusion
  156.0 1.0 copy.55
  157.0 0.0 copy-done
  157.0 0.0 copy-start.2
  157.1 2.8 %fusion.9 = (f32[1024]{0:T(1024)S(1)}, bf16[1024,1024]{0,1:T(8,128)(2,1)S(1)}) fusion(bf16[1,1024,1024]{2,1,0:T(8,128)(2,1)S(1)} %copy-done, bf16[128,8,8,128]{3,2,1,0:T(8,128)(2,1)S(1)} %bitcast.130, bf16[1024,1024]{0,1:T(8,128)(2,1)S(1)} %get-tuple-element.13), kind=kOutput, calls=%fused_computation.20 | convolution fusion | flops 2153774080 | bytes 8392704 | tf_op jit(solution)/shard_map/dot_general | solution.py:57
  159.9 0.0 copy-start.7
  159.9 1.4 copy-done.7
  161.2 0.0 copy-done.2
  161.2 7.0 %fusion.16 = f32[1024,2048]{1,0:T(8,128)} fusion(bf16[1,1024,2048]{2,1,0:T(8,128)(2,1)S(1)} %copy-done.2, bf16[1024,1024]{0,1:T(8,128)(2,1)S(1)} %get-tuple-element.17, f32[1024]{0:T(1024)S(1)} %bitcast.133, f32[1024]{0:T(1024)S(1)} %add_rsqrt_fusion.1), kind=kOutput, calls=%fused_computation.27 | convolution fusion | flops 4299161600 | bytes 14688256 | tf_op jit(solution)/shard_map/dot_general | solution.py:60
  168.2 0.0 copy-start.6
  168.3 18.4 %fusion.3 = (f32[1024]{0:T(1024)S(1)}, bf16[1024,1024]{0,1:T(8,128)(2,1)}) fusion(bf16[1,2048,1024]{2,1,0:T(8,128)(2,1)} %param.20, f32[1024,2048]{1,0:T(8,128)} %fusion.16, bf16[1,1024,2048]{2,1,0:T(8,128)(2,1)} %param.19, bf16[1024,1024]{0,1:T(8,128)(2,1)} %copy-done.7, f32[1024]{0:T(1024)S(1)} %bitcast.134, f32[1024]{0:T(1024)S(1)} %add_rsqrt_fusion.1), kind=kOutput, calls=%fused_computation.14 | convolution fusion | flops 8613002240 | bytes 20983808 | tf_op jit(solution)/shard_map/dot_general | solution.py:64
  186.7 0.0 copy-done.6
  186.7 2.4 %fusion.72 = bf16[1024,128]{1,0:T(8,128)(2,1)S(1)} fusion(bf16[1024,128]{1,0:T(8,128)(2,1)S(1)} %copy-done.6, bf16[1024,1024]{0,1:T(8,128)(2,1)} %get-tuple-element.19, f32[1024]{0:T(1024)S(1)} %add_rsqrt_fusion), kind=kOutput, calls=%fused_computation.72 | convolution fusion | flops 271712256 | bytes 2625536 | tf_op jit(solution)/shard_map/dot_general | solution.py:67
  189.1 0.3 copy.56
  189.4 8.5 %all_to_all.52 = bf16[2,2,256,128]{3,1,0,2:T(2,128)(2,1)S(1)} all-to-all(bf16[2,2,256,128]{3,1,0,2:T(2,128)(2,1)S(1)} %copy.56), channel_id=1, replica_groups=mesh['freq'=8,'tm'=16] {'freq'}, dimensions={2} | all-to-all | bytes 524288 | tf_op jit(solution)/shard_map/all_to_all | solution.py:115
  197.9 0.8 copy.57
  (6 shorter events, 0.0 us)
Async XLA Ops:
  0.0 157.0 %copy-start = (bf16[1,1024,1024]{2,1,0:T(8,128)(2,1)S(1)}, bf16[1,1024,1024]{2,1,0:T(8,128)(2,1)}, u32[]{:S(2)}) copy-start(bf16[1,1024,1024]{2,1,0:T(8,128)(2,1)} %param.16) | copy-start | bytes 6291460
  56.2 10.4 %copy-start.1 = (f32[1,2,1024]{2,1,0:T(2,128)S(1)}, f32[1,2,1024]{2,1,0:T(2,128)}, u32[]{:S(2)}) copy-start(f32[1,2,1024]{2,1,0:T(2,128)} %param.17) | copy-start | bytes 24580
  56.2 49.9 %all-to-all-start.1 = ((bf16[2,4,2,16,2,3072]{5,4,2,1,0,3:T(2,128)(2,1)}), bf16[2,4,2,16,2,3072]{5,4,2,1,0,3:T(2,128)(2,1)}, u32[]{:S(2)}, u32[]{:S(2)}) async-start(bf16[2,4,2,16,2,3072]{5,4,2,1,0,3:T(2,128)(2,1)} %all_to_all.40), calls=%async_computation.1 | async-start | bytes 6291456 | tf_op jit(solution)/shard_map/all_to_all | solution.py:92
  128.1 2.8 %copy-start.5 = (bf16[128,1024]{1,0:T(8,128)(2,1)S(1)}, bf16[128,1024]{1,0:T(8,128)(2,1)}, u32[]{:S(2)}) copy-start(bf16[128,1024]{1,0:T(8,128)(2,1)} %param.12) | copy-start | bytes 786436
  135.9 1.6 copy-start.3
  142.0 9.7 %copy-start.4 = (bf16[1,1024,1024]{2,1,0:T(8,128)(2,1)S(1)}, bf16[1,1024,1024]{2,1,0:T(8,128)(2,1)}, u32[]{:S(2)}) copy-start(bf16[1,1024,1024]{2,1,0:T(8,128)(2,1)} %param.15) | copy-start | bytes 6291460
  157.0 4.2 %copy-start.2 = (bf16[1,1024,2048]{2,1,0:T(8,128)(2,1)S(1)}, bf16[1,1024,2048]{2,1,0:T(8,128)(2,1)}, u32[]{:S(2)}) copy-start(bf16[1,1024,2048]{2,1,0:T(8,128)(2,1)} %param.18) | copy-start | bytes 12582916
  159.9 1.4 copy-start.7
  168.2 18.4 %copy-start.6 = (bf16[1024,128]{1,0:T(8,128)(2,1)S(1)}, bf16[1024,128]{1,0:T(8,128)(2,1)}, u32[]{:S(2)}) copy-start(bf16[1024,128]{1,0:T(8,128)(2,1)} %param.21) | copy-start | bytes 786436
where the time goes:
time: 200 us; the launch traced here: 199 us
  blocking collectives  51.3 us (26%)
  matrix products  50.1 us (25%)
  local copies, waits for them, and re-layouts  35.4 us (18%)
  other arithmetic  28.1 us (14%)
  waiting for transfers between devices  23.5 us (12%)
  starting transfers between devices  10.1 us (5%)
    all_to_all x1, blocking collectives, body(): lax.all_to_all(blocks, 'freq', split_axis=4, concat_axis=5, tiled=True)  42.8 us
    all_to_all x1, waiting for transfers between devices, body(): lax.all_to_all(lax.all_to_all(blocks, 'freq', split_axis=4, concat_axis=5...  23.5 us
    dot_general x1, matrix products, network(): jnp.dot(hidden, w_down[0], preferred_element_type=jnp.float32)  18.4 us
    another operation x3, other arithmetic  16.3 us
    all_to_all x2, local copies, waits for them, and re-layouts, body(): lax.all_to_all(blocks, 'freq', split_axis=4, concat_axis=5, tiled=True)  10.5 us
    all_to_all x1, starting transfers between devices, body(): lax.all_to_all(lax.all_to_all(blocks, 'freq', split_axis=4, concat_axis=5...  10.1 us
    sub x1, other arithmetic, network(): weights = jax.nn.softmax(scores, axis=-1).astype(jnp.bfloat16)  9.71 us
    all_to_all x1, blocking collectives, body(): lax.all_to_all(outcome, 'freq', split_axis=2, concat_axis=1, tiled=True)  8.52 us
  transfers between devices with their start and end apart: 1, of which 1 were waited for; matrix products, arithmetic and copies ran while one was open for 8% of the time, Pallas kernels for 0%

commit v1 on v0

v1 whole, which is shorter than its diff:
```python
import math

import jax
import jax.numpy as jnp
import ml_dtypes
import numpy as np
from jax import lax
from jax.experimental import pallas as pl
from jax.experimental.pallas import tpu as pltpu
from jax.sharding import PartitionSpec as P

BF = jnp.bfloat16
F32 = jnp.float32
MESH = pl.DeviceIdType.MESH

SUBCARRIERS = 3072
TAPS = 256
SLOTS = 64
TILE = 32
FREQ = 8
XN, YN = 2, 4
TM = 16
D = 1024
FF = 2048
CHUNKS = 4
ROWS = 256
BLOCK = 128
OFFSETS = [(dx, dy) for dx in (1, 0) for dy in (2, 1, 3, 0) if (dx, dy) != (0, 0)]


def dot(a, b):
    return jnp.dot(a, b, preferred_element_type=F32)


def delay_tables():
    share = SUBCARRIERS // FREQ
    f = np.arange(SUBCARRIERS)[:, None]
    t = np.arange(TAPS)[None, :]
    angle = 2.0 * math.pi / SUBCARRIERS * (f * t % SUBCARRIERS)
    r = 1.0 / math.sqrt(SUBCARRIERS)
    cosine, sine = np.cos(angle) * r, np.sin(angle) * r
    table = np.stack([np.stack([cosine, -sine], 1), np.stack([sine, cosine], 1)], 0)
    table = table.reshape(2, FREQ, share, 2, XN, YN, TILE)
    table = table.transpose(1, 0, 2, 5, 4, 3, 6)
    both = np.stack([table, table[:, :, :, :, ::-1]], 0)
    return both.reshape(2, FREQ, 2 * share, 2 * TAPS).astype(ml_dtypes.bfloat16)


def doppler_tables():
    s = np.arange(SLOTS)[:, None]
    k = np.arange(SLOTS)[None, :]
    angle = 2.0 * math.pi / SLOTS * (s * k % SLOTS)
    r = 1.0 / math.sqrt(SLOTS)
    cosine, sine = np.cos(angle) * r, np.sin(angle) * r
    table = np.stack([np.stack([cosine, -sine], 1), np.stack([sine, cosine], 1)], 0)
    table = table.reshape(2, TM, 2, 2, 2 * SLOTS)
    table = table.transpose(3, 0, 1, 2, 4)
    out = np.zeros((XN, 2, 2, 4, TM, 2, 4, 2 * SLOTS))
    for a in range(4):
        out[0, :, :, a, :, :, a] = table
        out[1, :, :, a, :, :, a] = table[::-1]
    return out.reshape(XN, 512, 512).astype(ml_dtypes.bfloat16)


def normed(x):
    return x * lax.rsqrt(jnp.mean(x * x, axis=-1, keepdims=True) + 1e-05)


def kernel(
    spectra, tables, doppler, w_embed, w_query, w_key, w_value, w_out, gains, w_gate, w_up, w_down, w_head,
    out,
    spec, tab_a, tab_b, dop, ve, vq, vk, vv, vo, vg, vu, vd, vh,
    part, got, taps, tiles, wide, feats, xs, hs, ms, hid,
    load_sem, part_send, part_recv, tile_send, tile_recv,
):
    freq = lax.axis_index("freq")
    tm = lax.axis_index("tm")
    mx, my = freq // YN, freq % YN

    loads = [
        (tables.at[0, freq], tab_a),
        (tables.at[1, freq], tab_b),
        (spectra.at[0], spec.at[0]),
        (spectra.at[1], spec.at[1]),
        (doppler.at[mx], dop),
        (w_embed, ve),
        (w_query.at[0], vq),
        (w_key.at[0], vk),
        (w_value.at[0], vv),
        (w_out.at[0], vo),
        (w_gate.at[0], vg),
        (w_up.at[0], vu),
        (w_down.at[0], vd),
        (w_head, vh),
    ]
    loads = [pltpu.make_async_copy(a, b, load_sem.at[i]) for i, (a, b) in enumerate(loads)]
    for load in loads:
        load.start()

    def peer(dx, dy):
        return (mx + dx) % XN * YN + (my + dy) % YN

    barrier = pltpu.get_barrier_semaphore()
    for dx, dy in OFFSETS:
        pl.semaphore_signal(barrier, inc=1, device_id={"freq": peer(dx, dy)}, device_id_type=MESH)

    def greet(i, _):
        pl.semaphore_signal(barrier, inc=1, device_id={"tm": (tm + i) % TM}, device_id_type=MESH)
        return 0

    lax.fori_loop(1, TM, greet, 0)

    low = lax.broadcasted_iota(jnp.int32, (ROWS, 128), 1) < 64

    def transform(u):
        for yp in range(2):
            cols = slice(256 * yp, 256 * yp + 256)
            sums = []
            for s in range(4):
                x = jnp.concatenate([spec[u, s, 0], spec[u, s, 1]], axis=1)
                sums.append(dot(x, (tab_b if s % 2 else tab_a)[:, cols]))
            for yy in range(2):
                a = [v[:, 128 * yy : 128 * yy + 128] for v in sums]
                for x in range(XN):
                    pair = [jnp.where(low, a[2 * sp + x], a[2 * sp + 1 - x]) for sp in range(2)]
                    pair = [v.reshape(TM, 2, 8, 128) for v in pair]
                    for ah in range(2):
                        rows = jnp.stack([pair[0][:, ah], pair[1][:, ah]], axis=1).reshape(ROWS, 128)
                        part[2 * u + ah, x * YN + 2 * yp + yy] = rows.astype(BF)

    def part_copy(c, i):
        dx, dy = OFFSETS[i]
        target = peer(dx, dy)
        return pltpu.make_async_remote_copy(
            src_ref=part.at[c, target],
            dst_ref=got.at[c, i],
            send_sem=part_send.at[c],
            recv_sem=part_recv.at[c],
            device_id={"freq": target},
            device_id_type=MESH,
        )

    def part_all(c):
        return pltpu.make_async_remote_copy(
            src_ref=part.at[c, pl.ds(0, FREQ - 1)],
            dst_ref=got.at[c],
            send_sem=part_send.at[c],
            recv_sem=part_recv.at[c],
            device_id={"freq": peer(0, 1)},
            device_id_type=MESH,
        )

    def tile_copy(c, i):
        target = (tm + i) % TM
        return pltpu.make_async_remote_copy(
            src_ref=taps.at[c, target],
            dst_ref=tiles.at[c, tm],
            send_sem=tile_send.at[c],
            recv_sem=tile_recv.at[c],
            device_id={"tm": target},
            device_id_type=MESH,
        )

    def tile_all(c):
        return pltpu.make_async_remote_copy(
            src_ref=taps.at[c, pl.ds(0, TM - 1)],
            dst_ref=tiles.at[c, pl.ds(0, TM - 1)],
            send_sem=tile_send.at[c],
            recv_sem=tile_recv.at[c],
            device_id={"tm": (tm + 1) % TM},
            device_id_type=MESH,
        )

    for i in range(3):
        loads[i].wait()
    transform(0)
    pl.semaphore_wait(barrier, FREQ - 1 + TM - 1)
    for c in (0, 1):
        for i in range(FREQ - 1):
            part_copy(c, i).start()
    loads[3].wait()
    transform(1)
    for c in (2, 3):
        for i in range(FREQ - 1):
            part_copy(c, i).start()

    def reduce(c):
        part_all(c).wait_recv()
        total = part[c, freq].astype(F32)
        for i in range(FREQ - 1):
            total = total + got[c, i].astype(F32)
        taps[c] = total.astype(BF).reshape(TM, 16, 128)

        def send(i, _):
            tile_copy(c, i).start()
            return 0

        lax.fori_loop(1, TM, send, 0)
        tiles[c, tm] = taps[c, tm]

    reduce(0)
    for load in loads[4:]:
        load.wait()

    same_tile = (
        lax.broadcasted_iota(jnp.int32, (BLOCK, BLOCK), 0) // TILE
        == lax.broadcasted_iota(jnp.int32, (BLOCK, BLOCK), 1) // TILE
    )
    spans = [(j, b) for j in range(2) for b in range(ROWS // BLOCK)]

    def doppler_of(c):
        tile_all(c).wait_recv()
        wide[...] = tiles[c].astype(F32).reshape(ROWS, 128)
        groups = []
        for g in range(2):
            stacked = jnp.concatenate([wide[pl.ds(4 * g + a, 32, stride=8), :] for a in range(4)], axis=0)
            turned = stacked.T.astype(BF)
            groups.append(jnp.concatenate([turned[32 * q : 32 * q + 32] for q in range(4)], axis=1))
        spread = dot(jnp.concatenate(groups, axis=0), dop[...]).astype(BF)
        for g in range(2):
            for a in range(4):
                first = 32 * (4 * g + a)
                feats[first : first + 32, :] = spread[32 * g : 32 * g + 32, 128 * a : 128 * a + 128]

    def norm_rows(gain):
        for r in range(0, ROWS, 64):
            rows = slice(r, r + 64)
            value = normed(xs[rows, :].astype(F32))
            hs[rows, :] = (value if gain is None else value * gains[0, gain : gain + 1, :]).astype(BF)

    def attend(hp, scores, v):
        scores = [jnp.where(same_tile, s, -1e30) for s in scores]
        tops = [jnp.max(s, axis=-1, keepdims=True) for s in scores]
        weights = [jnp.exp((s - m) * 128**-0.5) for s, m in zip(scores, tops)]
        sums = [jnp.sum(p, axis=-1, keepdims=True) for p in weights]
        weights = [(p * (1.0 / t)).astype(BF) for p, t in zip(weights, sums)]
        for p, (j, b) in zip(weights, spans):
            rows = slice(b * BLOCK, (b + 1) * BLOCK)
            first = hp * 256 + j * 128
            ms[rows, first : first + 128] = dot(p, v[rows, j * 128 : (j + 1) * 128]).astype(BF)

    def chunk(c, _):
        doppler_of(c)
        for n in range(0, D, 256):
            cols = slice(n, n + 256)
            xs[:, cols] = dot(feats[...], ve[:, cols]).astype(BF)
        norm_rows(0)
        waiting = []
        for hp in range(4):
            cols = slice(hp * 256, hp * 256 + 256)
            q = dot(hs[...], vq[:, cols]).astype(BF)
            k = dot(hs[...], vk[:, cols]).astype(BF)
            v = dot(hs[...], vv[:, cols]).astype(BF)
            scores = []
            for j, b in spans:
                rows, part_cols = slice(b * BLOCK, (b + 1) * BLOCK), slice(j * 128, (j + 1) * 128)
                scores.append(
                    lax.dot_general(
                        q[rows, part_cols], k[rows, part_cols], (((1,), (1,)), ((), ())), preferred_element_type=F32
                    )
                )
            waiting.append((hp, scores, v))
            if hp:
                attend(*waiting.pop(0))
        attend(*waiting.pop(0))
        for n in range(0, D, 256):
            cols = slice(n, n + 256)
            xs[:, cols] = (xs[:, cols].astype(F32) + dot(ms[...], vo[:, cols])).astype(BF)

        @pl.when(c < CHUNKS - 1)
        def _():
            reduce(c + 1)

        norm_rows(1)
        for n in range(0, FF, 256):
            cols = slice(n, n + 256)
            gate = dot(hs[...], vg[:, cols])
            up = dot(hs[...], vu[:, cols])
            hid[:, cols] = (jax.nn.silu(gate) * up).astype(BF)
        for n in range(0, D, 256):
            cols = slice(n, n + 256)
            xs[:, cols] = (xs[:, cols].astype(F32) + dot(hid[...], vd[:, cols])).astype(BF)
        norm_rows(None)
        out[c] = dot(hs[...], vh[...]).astype(BF)
        return 0

    lax.fori_loop(0, CHUNKS, chunk, 0)

    def drain(c, _):
        part_all(c).wait_send()
        tile_all(c).wait_send()
        return 0

    lax.fori_loop(0, CHUNKS, drain, 0)


def body(spectra, w_embed, w_query, w_key, w_value, w_out, norm_gains, w_gate, w_up, w_down, w_head):
    vmem, dma = pltpu.VMEM, pltpu.SemaphoreType.DMA
    hbm = pl.BlockSpec(memory_space=pl.ANY)
    near = pl.BlockSpec(memory_space=pltpu.VMEM)
    result = pl.pallas_call(
        kernel,
        out_shape=jax.ShapeDtypeStruct((CHUNKS, ROWS, 2 * SLOTS), BF),
        in_specs=[hbm] * 8 + [near] + [hbm] * 4,
        out_specs=near,
        scratch_shapes=[
            vmem((2, 4, 2, 256, 384), BF),
            vmem((768, 512), BF),
            vmem((768, 512), BF),
            vmem((512, 512), BF),
            vmem((2 * SLOTS, D), BF),
            vmem((D, D), BF),
            vmem((D, D), BF),
            vmem((D, D), BF),
            vmem((D, D), BF),
            vmem((D, FF), BF),
            vmem((D, FF), BF),
            vmem((FF, D), BF),
            vmem((D, 2 * SLOTS), BF),
            vmem((CHUNKS, FREQ, ROWS, 128), BF),
            vmem((CHUNKS, FREQ - 1, ROWS, 128), BF),
            vmem((CHUNKS, TM, 16, 128), BF),
            vmem((CHUNKS, TM, 16, 128), BF),
            vmem((ROWS, 128), F32),
            vmem((ROWS, 128), BF),
            vmem((ROWS, D), BF),
            vmem((ROWS, D), BF),
            vmem((ROWS, D), BF),
            vmem((ROWS, FF), BF),
            dma((14,)),
            dma((CHUNKS,)),
            dma((CHUNKS,)),
            dma((CHUNKS,)),
            dma((CHUNKS,)),
        ],
        compiler_params=pltpu.CompilerParams(collective_id=0, has_side_effects=True, vmem_limit_bytes=58 << 20),
        name="fused",
    )(
        spectra, jnp.asarray(delay_tables()), jnp.asarray(doppler_tables()),
        w_embed, w_query, w_key, w_value, w_out, norm_gains, w_gate, w_up, w_down, w_head,
    )
    return result.reshape(2, 16, TILE, 2 * SLOTS)


def solution(mesh):
    placed = (P(None, "tm", None, None, "freq"), P(), P(), P(), P(), P(), P(), P(), P(), P(), P())
    return jax.shard_map(
        body, mesh=mesh, in_specs=placed, out_specs=P(None, "tm", "freq", None), check_vma=False
    )
```

time: 200 us -> 71.6 us (0.36)
  Pallas kernels: 0 us -> 69.8 us
  blocking collectives: 51.3 us -> 0 us
  matrix products: 50.1 us -> 0 us
  local copies, waits for them, and re-layouts: 35.4 us -> 1.67 us
  other arithmetic: 28.1 us -> 0 us
  waiting for transfers between devices: 23.5 us -> 0 us
  starting transfers between devices: 10.1 us -> 0 us
    pallas_call x0 -> x1, Pallas kernels: none -> 69.8 us  [body(): pl.pallas_call(kernel, out_shape=jax.ShapeDtypeStruct((CHUNKS, ROWS, 2 *...]
    all_to_all x2 -> x0, blocking collectives: 51.3 us -> none  [the longest x1 42.8 us: body(): lax.all_to_all(blocks, 'freq', split_axis=4, concat_axis=5, tiled=True)]
    dot_general x12 -> x0, matrix products: 50.1 us -> none  [the longest x1 18.4 us: network(): jnp.dot(hidden, w_down[0], preferred_element_type=jnp.float32)]
    all_to_all x1 -> x0, waiting for transfers between devices: 23.5 us -> none  [body(): lax.all_to_all(lax.all_to_all(blocks, 'freq', split_axis=4, concat_axis=5...]
    all_to_all x4 -> x0, local copies, waits for them, and re-layouts: 18.6 us -> none  [the longest x2 10.5 us: body(): lax.all_to_all(blocks, 'freq', split_axis=4, concat_axis=5, tiled=True)]
    another operation x4 -> x0, other arithmetic: 16.3 us -> none
    reshape x4 -> x0, local copies, waits for them, and re-layouts: 11.3 us -> none  [the longest x1 8.01 us: body(): local = moved.reshape(users, slots, 2, -1, freq_count, sub_share)]
    all_to_all x1 -> x0, starting transfers between devices: 10.1 us -> none  [body(): lax.all_to_all(lax.all_to_all(blocks, 'freq', split_axis=4, concat_axis=5...]
  transfers between devices with their start and end apart: 1 -> 0, of which waited for: 1 -> 0; matrix products, arithmetic and copies ran while one was open for 8% -> 0% of each run, Pallas kernels for 0% -> 0%
where the time goes in v1:
time: 71.6 us; the launch traced here: 71.4 us
  Pallas kernels  69.8 us (97%)
  local copies, waits for them, and re-layouts  1.67 us (2%)
    pallas_call x1, Pallas kernels, body(): pl.pallas_call(kernel, out_shape=jax.ShapeDtypeStruct((CHUNKS, ROWS, 2 *...  69.8 us
    unnamed x1, local copies, waits for them, and re-layouts  1.67 us

profile of v1, /device:TPU:1, one launch (start us, length us, event | category | flops | bytes accessed | tf_op | source)
XLA Modules:
  0.0 71.4 jit_solution(8390155280558400785)
XLA Ops:
  0.0 69.8 %fused.1 = bf16[4,256,128]{2,1,0:T(8,128)(2,1)} custom-call(bf16[2,4,2,256,384]{4,3,2,1,0:T(8,128)(2,1)} %spectra.1, bf16[2,8,768,512]{3,2,1,0:T(8,128)(2,1)} %constant.4.clone.tables, bf16[2,512,512]{2,1,0:T(8,128)(2,1)} %constant.5.clone.doppler, bf16[128,1024]{1,0:T(8,128)(2,1)} %w_embed.1, bf16[1,1024,1024]{2,1,0:T(8,128)(2,1)} %w_query.1, ...), custom_call_target="tpu_custom_call" | custom-call | tf_op jit(solution)/shard_map/fused/pallas_call | solution.py:301
  69.8 1.7 %copy.15 = bf16[2,16,32,128]{3,2,1,0:T(8,128)(2,1)} copy(bf16[2,16,32,128]{3,2,1,0:T(8,128)(2,1)} %bitcast.1) | data formatting | bytes 524288

commit v2 on v1

--- a/solution.py
+++ b/solution.py
@@ -25,7 +25,7 @@
 CHUNKS = 4
 ROWS = 256
 BLOCK = 128
-OFFSETS = [(dx, dy) for dx in (1, 0) for dy in (2, 1, 3, 0) if (dx, dy) != (0, 0)]
+HALF = ROWS // 2
 
 
 def dot(a, b):
@@ -70,12 +70,12 @@
     spectra, tables, doppler, w_embed, w_query, w_key, w_value, w_out, gains, w_gate, w_up, w_down, w_head,
     out,
     spec, tab_a, tab_b, dop, ve, vq, vk, vv, vo, vg, vu, vd, vh,
-    part, got, taps, tiles, wide, feats, xs, hs, ms, hid,
-    load_sem, part_send, part_recv, tile_send, tile_recv,
+    part_a, part_b, got_a, got_b, sum_a, sum_b, last_a, last_b, taps, tiles, wide, feats, xs, hs, ms, hid,
+    load_sem, sends, recvs, meet,
 ):
     freq = lax.axis_index("freq")
     tm = lax.axis_index("tm")
-    mx, my = freq // YN, freq % YN
+    mx, my = lax.div(freq, YN), lax.rem(freq, YN)
 
     loads = [
         (tables.at[0, freq], tab_a),
@@ -94,21 +94,25 @@
         (w_head, vh),
     ]
     loads = [pltpu.make_async_copy(a, b, load_sem.at[i]) for i, (a, b) in enumerate(loads)]
-    for load in loads:
+    for load in loads[:3]:
         load.start()
 
-    def peer(dx, dy):
-        return (mx + dx) % XN * YN + (my + dy) % YN
-
+    other_x = (1 - mx) * YN + my
+
+    def along_y(i):
+        return lax.rem(my + 1 + i, YN)
+
+    tz, th, tc = lax.div(tm, 4), lax.rem(lax.div(tm, 2), 2), lax.rem(tm, 2)
+    other_h = tz * 4 + (1 - th) * 2 + tc
+    other_c = tz * 4 + th * 2 + (1 - tc)
     barrier = pltpu.get_barrier_semaphore()
-    for dx, dy in OFFSETS:
-        pl.semaphore_signal(barrier, inc=1, device_id={"freq": peer(dx, dy)}, device_id_type=MESH)
-
-    def greet(i, _):
-        pl.semaphore_signal(barrier, inc=1, device_id={"tm": (tm + i) % TM}, device_id_type=MESH)
-        return 0
-
-    lax.fori_loop(1, TM, greet, 0)
+    for i in range(YN - 1):
+        pl.semaphore_signal(barrier, inc=1, device_id={"freq": mx * YN + along_y(i)}, device_id_type=MESH)
+    pl.semaphore_signal(barrier, inc=1, device_id={"freq": other_x}, device_id_type=MESH)
+    for i in range(1, 4):
+        pl.semaphore_signal(barrier, inc=1, device_id={"tm": lax.rem(tm + 4 * i, TM)}, device_id_type=MESH)
+    for other in (other_h, other_c):
+        pl.semaphore_signal(barrier, inc=1, device_id={"tm": other}, device_id_type=MESH)
 
     low = lax.broadcasted_iota(jnp.int32, (ROWS, 128), 1) < 64
 
@@ -126,79 +130,103 @@
                     pair = [v.reshape(TM, 2, 8, 128) for v in pair]
                     for ah in range(2):
                         rows = jnp.stack([pair[0][:, ah], pair[1][:, ah]], axis=1).reshape(ROWS, 128)
-                        part[2 * u + ah, x * YN + 2 * yp + yy] = rows.astype(BF)
-
-    def part_copy(c, i):
-        dx, dy = OFFSETS[i]
-        target = peer(dx, dy)
+                        part_a[2 * u + ah, 2 * yp + yy, x] = rows[:HALF].astype(BF)
+                        part_b[2 * u + ah, x, 2 * yp + yy] = rows[HALF:].astype(BF)
+
+    def remote(src, dst, kind, c, device):
         return pltpu.make_async_remote_copy(
-            src_ref=part.at[c, target],
-            dst_ref=got.at[c, i],
-            send_sem=part_send.at[c],
-            recv_sem=part_recv.at[c],
-            device_id={"freq": target},
+            src_ref=src,
+            dst_ref=dst,
+            send_sem=sends.at[kind, c],
+            recv_sem=recvs.at[kind, c],
+            device_id=device,
             device_id_type=MESH,
         )
 
-    def part_all(c):
-        return pltpu.make_async_remote_copy(
-            src_ref=part.at[c, pl.ds(0, FREQ - 1)],
-            dst_ref=got.at[c],
-            send_sem=part_send.at[c],
-            recv_sem=part_recv.at[c],
-            device_id={"freq": peer(0, 1)},
-            device_id_type=MESH,
-        )
-
-    def tile_copy(c, i):
-        target = (tm + i) % TM
-        return pltpu.make_async_remote_copy(
-            src_ref=taps.at[c, target],
-            dst_ref=tiles.at[c, tm],
-            send_sem=tile_send.at[c],
-            recv_sem=tile_recv.at[c],
-            device_id={"tm": target},
-            device_id_type=MESH,
-        )
-
-    def tile_all(c):
-        return pltpu.make_async_remote_copy(
-            src_ref=taps.at[c, pl.ds(0, TM - 1)],
-            dst_ref=tiles.at[c, pl.ds(0, TM - 1)],
-            send_sem=tile_send.at[c],
-            recv_sem=tile_recv.at[c],
-            device_id={"tm": (tm + 1) % TM},
-            device_id_type=MESH,
-        )
-
-    for i in range(3):
-        loads[i].wait()
+    near_x = {"freq": other_x}
+
+    def copy_a(c, i):
+        y = along_y(i)
+        return remote(part_a.at[c, y], got_a.at[c, i], 0, c, {"freq": mx * YN + y})
+
+    def copy_b(c):
+        return remote(part_b.at[c, 1 - mx], got_b.at[c], 1, c, near_x)
+
+    def copy_sum_a(c):
+        return remote(sum_a.at[c, 1 - mx], last_a.at[c], 2, c, near_x)
+
+    def copy_sum_b(c, i):
+        y = along_y(i)
+        return remote(sum_b.at[c, y], last_b.at[c, i], 3, c, {"freq": mx * YN + y})
+
+    def all_a(c):
+        return remote(part_a.at[c, pl.ds(0, YN - 1)], got_a.at[c], 0, c, near_x)
+
+    def all_sum_b(c):
+        return remote(sum_b.at[c, pl.ds(0, YN - 1)], last_b.at[c], 3, c, near_x)
+
+    def start_parts(c):
+        copy_b(c).start()
+        for i in (1, 0, 2):
+            copy_a(c, i).start()
+
+    def middle(c):
+        all_a(c).wait_recv()
+        for x in range(XN):
+            total = part_a[c, my, x].astype(F32)
+            for i in range(YN - 1):
+                total = total + got_a[c, i, x].astype(F32)
+            sum_a[c, x] = total.astype(BF)
+        copy_sum_a(c).start()
+        copy_b(c).wait_recv()
+        for y in range(YN):
+            sum_b[c, y] = (part_b[c, mx, y].astype(F32) + got_b[c, y].astype(F32)).astype(BF)
+        for i in (1, 0, 2):
+            copy_sum_b(c, i).start()
+
+    def copy_tile(c, i):
+        target = lax.rem(tm + i, TM)
+        return remote(taps.at[c, target], tiles.at[c, tm], 4, c, {"tm": target})
+
+    def all_tiles(c):
+        return remote(taps.at[c, pl.ds(0, TM - 1)], tiles.at[c, pl.ds(0, TM - 1)], 4, c, {"tm": other_c})
+
+    for load in loads[:3]:
+        load.wait()
+    for load in loads[3:]:
+        load.start()
     transform(0)
-    pl.semaphore_wait(barrier, FREQ - 1 + TM - 1)
-    for c in (0, 1):
-        for i in range(FREQ - 1):
-            part_copy(c, i).start()
+    pl.semaphore_wait(barrier, 9)
+    start_parts(0)
+    pl.semaphore_signal(meet.at[0], inc=1, device_id={"tm": other_h}, device_id_type=MESH)
     loads[3].wait()
     transform(1)
-    for c in (2, 3):
-        for i in range(FREQ - 1):
-            part_copy(c, i).start()
+    pl.semaphore_wait(meet.at[0], 1)
+    pl.semaphore_signal(meet.at[1], inc=1, device_id={"tm": other_c}, device_id_type=MESH)
+    pl.semaphore_wait(meet.at[1], 1)
 
     def reduce(c):
-        part_all(c).wait_recv()
-        total = part[c, freq].astype(F32)
-        for i in range(FREQ - 1):
-            total = total + got[c, i].astype(F32)
-        taps[c] = total.astype(BF).reshape(TM, 16, 128)
+        copy_sum_a(c).wait_recv()
+        taps[c, 0:8] = (sum_a[c, mx].astype(F32) + last_a[c].astype(F32)).astype(BF).reshape(TM // 2, 16, 128)
+        all_sum_b(c).wait_recv()
+        total = sum_b[c, my].astype(F32)
+        for i in range(YN - 1):
+            total = total + last_b[c, i].astype(F32)
+        taps[c, 8:16] = total.astype(BF).reshape(TM // 2, 16, 128)
 
         def send(i, _):
-            tile_copy(c, i).start()
+            copy_tile(c, i).start()
             return 0
 
         lax.fori_loop(1, TM, send, 0)
         tiles[c, tm] = taps[c, tm]
 
+    middle(0)
+    start_parts(1)
     reduce(0)
+    middle(1)
+    start_parts(2)
+    start_parts(3)
     for load in loads[4:]:
         load.wait()
 
@@ -209,7 +237,7 @@
     spans = [(j, b) for j in range(2) for b in range(ROWS // BLOCK)]
 
     def doppler_of(c):
-        tile_all(c).wait_recv()
+        all_tiles(c).wait_recv()
         wide[...] = tiles[c].astype(F32).reshape(ROWS, 128)
         groups = []
         for g in range(2):
@@ -241,6 +269,7 @@
 
     def chunk(c, _):
         doppler_of(c)
+        pl.when(c < CHUNKS - 1)(lambda: reduce(c + 1))
         for n in range(0, D, 256):
             cols = slice(n, n + 256)
             xs[:, cols] = dot(feats[...], ve[:, cols]).astype(BF)
@@ -267,9 +296,7 @@
             cols = slice(n, n + 256)
             xs[:, cols] = (xs[:, cols].astype(F32) + dot(ms[...], vo[:, cols])).astype(BF)
 
-        @pl.when(c < CHUNKS - 1)
-        def _():
-            reduce(c + 1)
+        pl.when(c < CHUNKS - 2)(lambda: middle(c + 2))
 
         norm_rows(1)
         for n in range(0, FF, 256):
@@ -287,8 +314,11 @@
     lax.fori_loop(0, CHUNKS, chunk, 0)
 
     def drain(c, _):
-        part_all(c).wait_send()
-        tile_all(c).wait_send()
+        all_a(c).wait_send()
+        copy_b(c).wait_send()
+        copy_sum_a(c).wait_send()
+        all_sum_b(c).wait_send()
+        all_tiles(c).wait_send()
         return 0
 
     lax.fori_loop(0, CHUNKS, drain, 0)
@@ -317,8 +347,14 @@
             vmem((D, FF), BF),
             vmem((FF, D), BF),
             vmem((D, 2 * SLOTS), BF),
-            vmem((CHUNKS, FREQ, ROWS, 128), BF),
-            vmem((CHUNKS, FREQ - 1, ROWS, 128), BF),
+            vmem((CHUNKS, YN, XN, HALF, 128), BF),
+            vmem((CHUNKS, XN, YN, HALF, 128), BF),
+            vmem((CHUNKS, YN - 1, XN, HALF, 128), BF),
+            vmem((CHUNKS, YN, HALF, 128), BF),
+            vmem((CHUNKS, XN, HALF, 128), BF),
+            vmem((CHUNKS, YN, HALF, 128), BF),
+            vmem((CHUNKS, HALF, 128), BF),
+            vmem((CHUNKS, YN - 1, HALF, 128), BF),
             vmem((CHUNKS, TM, 16, 128), BF),
             vmem((CHUNKS, TM, 16, 128), BF),
             vmem((ROWS, 128), F32),
@@ -328,10 +364,9 @@
             vmem((ROWS, D), BF),
             vmem((ROWS, FF), BF),
             dma((14,)),
-            dma((CHUNKS,)),
-            dma((CHUNKS,)),
-            dma((CHUNKS,)),
-            dma((CHUNKS,)),
+            dma((5, CHUNKS)),
+            dma((5, CHUNKS)),
+            pltpu.SemaphoreType.REGULAR((2,)),
         ],
         compiler_params=pltpu.CompilerParams(collective_id=0, has_side_effects=True, vmem_limit_bytes=58 << 20),
         name="fused",

time: 71.6 us -> 58.3 us (0.81)
  Pallas kernels: 69.8 us -> 56.4 us
    pallas_call x1, Pallas kernels: 69.8 us -> 56.4 us  [body(): pl.pallas_call(kernel, out_shape=jax.ShapeDtypeStruct((CHUNKS, ROWS, 2 *...]
where the time goes in v2:
time: 58.3 us; the launch traced here: 58.1 us
  Pallas kernels  56.4 us (97%)
  local copies, waits for them, and re-layouts  1.67 us (3%)
    pallas_call x1, Pallas kernels, body(): pl.pallas_call(kernel, out_shape=jax.ShapeDtypeStruct((CHUNKS, ROWS, 2 *...  56.4 us
    unnamed x1, local copies, waits for them, and re-layouts  1.67 us

profile of v2, /device:TPU:1, one launch (start us, length us, event | category | flops | bytes accessed | tf_op | source)
XLA Modules:
  0.0 58.1 jit_solution(17814095267211454524)
XLA Ops:
  0.0 56.4 %fused.1 = bf16[4,256,128]{2,1,0:T(8,128)(2,1)} custom-call(bf16[2,4,2,256,384]{4,3,2,1,0:T(8,128)(2,1)} %spectra.1, bf16[2,8,768,512]{3,2,1,0:T(8,128)(2,1)} %constant.4.clone.tables, bf16[2,512,512]{2,1,0:T(8,128)(2,1)} %constant.5.clone.doppler, bf16[128,1024]{1,0:T(8,128)(2,1)} %w_embed.1, bf16[1,1024,1024]{2,1,0:T(8,128)(2,1)} %w_query.1, ...), custom_call_target="tpu_custom_call" | custom-call | tf_op jit(solution)/shard_map/fused/pallas_call | solution.py:331
  56.4 1.7 %copy.15 = bf16[2,16,32,128]{3,2,1,0:T(8,128)(2,1)} copy(bf16[2,16,32,128]{3,2,1,0:T(8,128)(2,1)} %bitcast.1) | data formatting | bytes 524288

commit v3 on v2

--- a/solution.py
+++ b/solution.py
@@ -21,6 +21,7 @@
 XN, YN = 2, 4
 TM = 16
 D = 1024
+HEADS = 8
 FF = 2048
 CHUNKS = 4
 ROWS = 256
@@ -30,6 +31,10 @@
 
 def dot(a, b):
     return jnp.dot(a, b, preferred_element_type=F32)
+
+
+def dot_t(a, b):
+    return lax.dot_general(a, b, (((1,), (1,)), ((), ())), preferred_element_type=F32)
 
 
 def delay_tables():
@@ -71,7 +76,7 @@
     out,
     spec, tab_a, tab_b, dop, ve, vq, vk, vv, vo, vg, vu, vd, vh,
     part_a, part_b, got_a, got_b, sum_a, sum_b, last_a, last_b, taps, tiles, wide, feats, xs, hs, ms, hid,
-    load_sem, sends, recvs, meet,
+    weg, pq, pk, pv, score_map, value_map, load_sem, sends, recvs, meet,
 ):
     freq = lax.axis_index("freq")
     tm = lax.axis_index("tm")
@@ -221,21 +226,48 @@
         lax.fori_loop(1, TM, send, 0)
         tiles[c, tm] = taps[c, tm]
 
+    def parts_left(c):
+        all_a(c).wait_send()
+        copy_b(c).wait_send()
+
+    def fold_inputs():
+        for load in loads[5:9]:
+            load.wait()
+        weg[...] = (ve[...].astype(F32) * gains[0, 0:1, :]).astype(BF)
+        for n in range(0, D, 256):
+            cols = slice(n, n + 256)
+            pq[:, cols] = dot(weg[...], vq[:, cols]).astype(BF)
+            pk[:, cols] = dot(weg[...], vk[:, cols]).astype(BF)
+            pv[:, cols] = dot(weg[...], vv[:, cols]).astype(BF)
+
+    def fold_heads():
+        loads[9].wait()
+        for h in range(HEADS):
+            cols = slice(h * 128, h * 128 + 128)
+            score_map[:, cols] = dot_t(pq[:, cols], pk[:, cols]).astype(BF)
+            value_map[cols, :] = dot(pv[:, cols], vo[cols, :]).astype(BF)
+
+    parts_left(0)
+    start_parts(1)
     middle(0)
-    start_parts(1)
+    parts_left(1)
+    start_parts(2)
     reduce(0)
+    fold_inputs()
     middle(1)
-    start_parts(2)
+    parts_left(2)
     start_parts(3)
-    for load in loads[4:]:
+    fold_heads()
+    middle(2)
+    reduce(1)
+    loads[4].wait()
+    for load in loads[10:]:
         load.wait()
 
     same_tile = (
         lax.broadcasted_iota(jnp.int32, (BLOCK, BLOCK), 0) // TILE
         == lax.broadcasted_iota(jnp.int32, (BLOCK, BLOCK), 1) // TILE
     )
-    spans = [(j, b) for j in range(2) for b in range(ROWS // BLOCK)]
-
     def doppler_of(c):
         all_tiles(c).wait_recv()
         wide[...] = tiles[c].astype(F32).reshape(ROWS, 128)
@@ -256,47 +288,57 @@
             value = normed(xs[rows, :].astype(F32))
             hs[rows, :] = (value if gain is None else value * gains[0, gain : gain + 1, :]).astype(BF)
 
-    def attend(hp, scores, v):
-        scores = [jnp.where(same_tile, s, -1e30) for s in scores]
-        tops = [jnp.max(s, axis=-1, keepdims=True) for s in scores]
-        weights = [jnp.exp((s - m) * 128**-0.5) for s, m in zip(scores, tops)]
+    def attend(heads, scores, both):
+        halves = [jnp.where(same_tile, v, -1e30) for s in scores for v in (s[:, :BLOCK], s[:, BLOCK:])]
+        tops = [jnp.max(s, axis=-1, keepdims=True) for s in halves]
+        weights = [jnp.exp((s - m) * 128**-0.5) for s, m in zip(halves, tops)]
         sums = [jnp.sum(p, axis=-1, keepdims=True) for p in weights]
         weights = [(p * (1.0 / t)).astype(BF) for p, t in zip(weights, sums)]
-        for p, (j, b) in zip(weights, spans):
-            rows = slice(b * BLOCK, (b + 1) * BLOCK)
-            first = hp * 256 + j * 128
-            ms[rows, first : first + 128] = dot(p, v[rows, j * 128 : (j + 1) * 128]).astype(BF)
+        for i, h in enumerate(heads):
+            mixed = dot(jnp.concatenate(weights[2 * i : 2 * i + 2], axis=1), both).astype(BF)
+            ms[:BLOCK, h * 128 : h * 128 + 128] = mixed[:, :128]
+            ms[BLOCK:, h * 128 : h * 128 + 128] = mixed[:, 128:]
 
     def chunk(c, _):
         doppler_of(c)
-        pl.when(c < CHUNKS - 1)(lambda: reduce(c + 1))
         for n in range(0, D, 256):
             cols = slice(n, n + 256)
             xs[:, cols] = dot(feats[...], ve[:, cols]).astype(BF)
-        norm_rows(0)
+        squares = None
+        for n in range(0, D, 128):
+            v = xs[:, n : n + 128].astype(F32)
+            squares = v * v if squares is None else squares + v * v
+        factor = lax.rsqrt(jnp.sum(squares, axis=-1, keepdims=True) * (1.0 / D) + 1e-05)
+        scaled = (feats[...].astype(F32) * factor).astype(BF)
+        for n in range(0, D, 256):
+            cols = slice(n, n + 256)
+            hs[:, cols] = dot(scaled, score_map[:, cols]).astype(BF)
+        zero = jnp.zeros((BLOCK, 128), BF)
+        both = jnp.concatenate(
+            [
+                jnp.concatenate([scaled[:BLOCK], zero], axis=1),
+                jnp.concatenate([zero, scaled[BLOCK:]], axis=1),
+            ],
+            axis=0,
+        )
         waiting = []
-        for hp in range(4):
-            cols = slice(hp * 256, hp * 256 + 256)
-            q = dot(hs[...], vq[:, cols]).astype(BF)
-            k = dot(hs[...], vk[:, cols]).astype(BF)
-            v = dot(hs[...], vv[:, cols]).astype(BF)
-            scores = []
-            for j, b in spans:
-                rows, part_cols = slice(b * BLOCK, (b + 1) * BLOCK), slice(j * 128, (j + 1) * 128)
-                scores.append(
-                    lax.dot_general(
-                        q[rows, part_cols], k[rows, part_cols], (((1,), (1,)), ((), ())), preferred_element_type=F32
-                    )
-                )
-            waiting.append((hp, scores, v))
-            if hp:
-                attend(*waiting.pop(0))
-        attend(*waiting.pop(0))
+        for first in range(0, HEADS, 2):
+            heads, scores = (first, first + 1), []
+            for h in heads:
+                cols = slice(h * 128, h * 128 + 128)
+                scores.append(dot_t(jnp.concatenate([hs[:BLOCK, cols], hs[BLOCK:, cols]], axis=1), both))
+            waiting.append((heads, scores))
+            if first:
+                attend(*waiting.pop(0), both)
+        attend(*waiting.pop(0), both)
+
+        pl.when(c < CHUNKS - 2)(lambda: reduce(c + 2))
+
         for n in range(0, D, 256):
             cols = slice(n, n + 256)
-            xs[:, cols] = (xs[:, cols].astype(F32) + dot(ms[...], vo[:, cols])).astype(BF)
-
-        pl.when(c < CHUNKS - 2)(lambda: middle(c + 2))
+            xs[:, cols] = (xs[:, cols].astype(F32) + dot(ms[...], value_map[:, cols])).astype(BF)
+
+        pl.when(c < CHUNKS - 3)(lambda: middle(c + 3))
 
         norm_rows(1)
         for n in range(0, FF, 256):
@@ -314,13 +356,12 @@
     lax.fori_loop(0, CHUNKS, chunk, 0)
 
     def drain(c, _):
-        all_a(c).wait_send()
-        copy_b(c).wait_send()
         copy_sum_a(c).wait_send()
         all_sum_b(c).wait_send()
         all_tiles(c).wait_send()
         return 0
 
+    parts_left(CHUNKS - 1)
     lax.fori_loop(0, CHUNKS, drain, 0)
 
 
@@ -363,6 +404,12 @@
             vmem((ROWS, D), BF),
             vmem((ROWS, D), BF),
             vmem((ROWS, FF), BF),
+            vmem((2 * SLOTS, D), BF),
+            vmem((2 * SLOTS, D), BF),
+            vmem((2 * SLOTS, D), BF),
+            vmem((2 * SLOTS, D), BF),
+            vmem((2 * SLOTS, D), BF),
+            vmem((D, D), BF),
             dma((14,)),
             dma((5, CHUNKS)),
             dma((5, CHUNKS)),

time: 58.3 us -> 54.1 us (0.928)
  Pallas kernels: 56.4 us -> 52.2 us
    pallas_call x1, Pallas kernels: 56.4 us -> 52.2 us  [body(): pl.pallas_call(kernel, out_shape=jax.ShapeDtypeStruct((CHUNKS, ROWS, 2 *...]
where the time goes in v3:
time: 54.1 us; the launch traced here: 53.9 us
  Pallas kernels  52.2 us (96%)
  local copies, waits for them, and re-layouts  1.67 us (3%)
    pallas_call x1, Pallas kernels, body(): pl.pallas_call(kernel, out_shape=jax.ShapeDtypeStruct((CHUNKS, ROWS, 2 *...  52.2 us
    unnamed x1, local copies, waits for them, and re-layouts  1.67 us

profile of v3, /device:TPU:1, one launch (start us, length us, event | category | flops | bytes accessed | tf_op | source)
XLA Modules:
  0.0 53.9 jit_solution(18256040119810465804)
XLA Ops:
  0.0 52.2 %fused.1 = bf16[4,256,128]{2,1,0:T(8,128)(2,1)} custom-call(bf16[2,4,2,256,384]{4,3,2,1,0:T(8,128)(2,1)} %spectra.1, bf16[2,8,768,512]{3,2,1,0:T(8,128)(2,1)} %constant.4.clone.tables, bf16[2,512,512]{2,1,0:T(8,128)(2,1)} %constant.5.clone.doppler, bf16[128,1024]{1,0:T(8,128)(2,1)} %w_embed.1, bf16[1,1024,1024]{2,1,0:T(8,128)(2,1)} %w_query.1, ...), custom_call_target="tpu_custom_call" | custom-call | tf_op jit(solution)/shard_map/fused/pallas_call | solution.py:372
  52.3 1.7 %copy.15 = bf16[2,16,32,128]{3,2,1,0:T(8,128)(2,1)} copy(bf16[2,16,32,128]{3,2,1,0:T(8,128)(2,1)} %bitcast.1) | data formatting | bytes 524288

commit v4 on v3

--- a/solution.py
+++ b/solution.py
@@ -1,3 +1,4 @@
+import functools
 import math
 
 import jax
@@ -22,6 +23,7 @@
 TM = 16
 D = 1024
 HEADS = 8
+SCORE_SCALE = 128**-0.5 * math.log2(math.e)
 FF = 2048
 CHUNKS = 4
 ROWS = 256
@@ -75,7 +77,7 @@
     spectra, tables, doppler, w_embed, w_query, w_key, w_value, w_out, gains, w_gate, w_up, w_down, w_head,
     out,
     spec, tab_a, tab_b, dop, ve, vq, vk, vv, vo, vg, vu, vd, vh,
-    part_a, part_b, got_a, got_b, sum_a, sum_b, last_a, last_b, taps, tiles, wide, feats, xs, hs, ms, hid,
+    part_a, part_b, got_a, got_b, sum_a, sum_b, last_a, last_b, taps, tiles, wide, feats, xs, hs, ms, hid, xb, h2, fin,
     weg, pq, pk, pv, score_map, value_map, load_sem, sends, recvs, meet,
 ):
     freq = lax.axis_index("freq")
@@ -244,7 +246,7 @@
         loads[9].wait()
         for h in range(HEADS):
             cols = slice(h * 128, h * 128 + 128)
-            score_map[:, cols] = dot_t(pq[:, cols], pk[:, cols]).astype(BF)
+            score_map[:, cols] = (dot_t(pq[:, cols], pk[:, cols]) * SCORE_SCALE).astype(BF)
             value_map[cols, :] = dot(pv[:, cols], vo[cols, :]).astype(BF)
 
     parts_left(0)
@@ -253,12 +255,11 @@
     parts_left(1)
     start_parts(2)
     reduce(0)
-    fold_inputs()
     middle(1)
     parts_left(2)
     start_parts(3)
+    fold_inputs()
     fold_heads()
-    middle(2)
     reduce(1)
     loads[4].wait()
     for load in loads[10:]:
@@ -282,78 +283,122 @@
                 first = 32 * (4 * g + a)
                 feats[first : first + 32, :] = spread[32 * g : 32 * g + 32, 128 * a : 128 * a + 128]
 
-    def norm_rows(gain):
-        for r in range(0, ROWS, 64):
-            rows = slice(r, r + 64)
-            value = normed(xs[rows, :].astype(F32))
-            hs[rows, :] = (value if gain is None else value * gains[0, gain : gain + 1, :]).astype(BF)
-
-    def attend(heads, scores, both):
-        halves = [jnp.where(same_tile, v, -1e30) for s in scores for v in (s[:, :BLOCK], s[:, BLOCK:])]
-        tops = [jnp.max(s, axis=-1, keepdims=True) for s in halves]
-        weights = [jnp.exp((s - m) * 128**-0.5) for s, m in zip(halves, tops)]
-        sums = [jnp.sum(p, axis=-1, keepdims=True) for p in weights]
-        weights = [(p * (1.0 / t)).astype(BF) for p, t in zip(weights, sums)]
-        for i, h in enumerate(heads):
-            mixed = dot(jnp.concatenate(weights[2 * i : 2 * i + 2], axis=1), both).astype(BF)
-            ms[:BLOCK, h * 128 : h * 128 + 128] = mixed[:, :128]
-            ms[BLOCK:, h * 128 : h * 128 + 128] = mixed[:, 128:]
-
-    def chunk(c, _):
+    def interleave(*lists):
+        steps = [((n + 0.5) / len(one), k, step) for k, one in enumerate(lists) for n, step in enumerate(one)]
+        for _, _, step in sorted(steps, key=lambda entry: entry[:2]):
+            step()
+
+    def norm_steps(target, read, gain):
+        def step(first):
+            rows = slice(first, first + 64)
+            value = normed(read(rows).astype(F32))
+            target[rows, :] = (value if gain is None else value * gains[0, gain : gain + 1, :]).astype(BF)
+
+        return [functools.partial(step, first) for first in range(0, ROWS, 64)]
+
+    def enter(c):
         doppler_of(c)
+        squares = None
         for n in range(0, D, 256):
             cols = slice(n, n + 256)
-            xs[:, cols] = dot(feats[...], ve[:, cols]).astype(BF)
-        squares = None
-        for n in range(0, D, 128):
-            v = xs[:, n : n + 128].astype(F32)
-            squares = v * v if squares is None else squares + v * v
+            x = dot(feats[...], ve[:, cols]).astype(BF)
+            xs[:, cols] = x
+            v = x.astype(F32)
+            v = v * v
+            v = v[:, :128] + v[:, 128:]
+            squares = v if squares is None else squares + v
         factor = lax.rsqrt(jnp.sum(squares, axis=-1, keepdims=True) * (1.0 / D) + 1e-05)
         scaled = (feats[...].astype(F32) * factor).astype(BF)
         for n in range(0, D, 256):
             cols = slice(n, n + 256)
             hs[:, cols] = dot(scaled, score_map[:, cols]).astype(BF)
         zero = jnp.zeros((BLOCK, 128), BF)
-        both = jnp.concatenate(
+        return jnp.concatenate(
             [
                 jnp.concatenate([scaled[:BLOCK], zero], axis=1),
                 jnp.concatenate([zero, scaled[BLOCK:]], axis=1),
             ],
             axis=0,
         )
-        waiting = []
-        for first in range(0, HEADS, 2):
-            heads, scores = (first, first + 1), []
-            for h in heads:
-                cols = slice(h * 128, h * 128 + 128)
-                scores.append(dot_t(jnp.concatenate([hs[:BLOCK, cols], hs[BLOCK:, cols]], axis=1), both))
-            waiting.append((heads, scores))
-            if first:
-                attend(*waiting.pop(0), both)
-        attend(*waiting.pop(0), both)
-
+
+    def attention_steps(both):
+        held = {}
+
+        def score(h):
+            cols = slice(h * 128, h * 128 + 128)
+            held[h] = dot_t(jnp.concatenate([hs[:BLOCK, cols], hs[BLOCK:, cols]], axis=1), both)
+
+        def top(h):
+            halves = [jnp.where(same_tile, v, -1e30) for v in (held[h][:, :BLOCK], held[h][:, BLOCK:])]
+            held[h] = [v - jnp.max(v, axis=-1, keepdims=True) for v in halves]
+
+        def power(h):
+            weights = [jnp.exp2(v) for v in held[h]]
+            sums = [jnp.sum(p, axis=-1, keepdims=True) for p in weights]
+            held[h] = (jnp.concatenate([p.astype(BF) for p in weights], axis=1), [1.0 / t for t in sums])
+
+        def mix(h):
+            weights, factors = held.pop(h)
+            mixed = dot(weights, both)
+            cols = slice(h * 128, h * 128 + 128)
+            ms[:BLOCK, cols] = (mixed[:, :128] * factors[0]).astype(BF)
+            ms[BLOCK:, cols] = (mixed[:, 128:] * factors[1]).astype(BF)
+
+        steps = []
+        for pair in range(HEADS // 2 + 1):
+            for kind, back in ((score, 0), (top, 1), (power, 1), (mix, 1)):
+                for h in (2 * (pair - back), 2 * (pair - back) + 1):
+                    if 0 <= h < HEADS:
+                        steps.append(functools.partial(kind, h))
+        return steps
+
+    def leave_attention(slot):
+        for n in range(0, D, 256):
+            cols = slice(n, n + 256)
+            xb[slot, :, cols] = (xs[:, cols].astype(F32) + dot(ms[...], value_map[:, cols])).astype(BF)
+
+    def gate_steps():
+        def step(n):
+            cols = slice(n, n + 256)
+            gate = dot(h2[...], vg[:, cols])
+            up = dot(h2[...], vu[:, cols])
+            hid[:, cols] = (jax.nn.silu(gate) * up).astype(BF)
+
+        return [functools.partial(step, n) for n in range(0, FF, 256)]
+
+    def down_steps(slot):
+        def step(n):
+            cols = slice(n, n + 256)
+            fin[:, cols] = (xb[slot, :, cols].astype(F32) + dot(hid[...], vd[:, cols])).astype(BF)
+
+        return [functools.partial(step, n) for n in range(0, D, 256)]
+
+    def finish(c):
+        interleave(norm_steps(hs, lambda rows: fin[rows, :], None))
+        out[c] = dot(hs[...], vh[...]).astype(BF)
+
+    interleave(attention_steps(enter(0)))
+    middle(2)
+    leave_attention(0)
+    interleave(norm_steps(h2, lambda rows: xb[0, rows, :], 1))
+
+    def chunk(c, _):
+        slot = lax.rem(c, 2)
+        pl.when(c < CHUNKS - 3)(lambda: middle(c + 3))
+        gates = gate_steps()
+        interleave(gates[:4])
+        both = enter(c + 1)
         pl.when(c < CHUNKS - 2)(lambda: reduce(c + 2))
-
-        for n in range(0, D, 256):
-            cols = slice(n, n + 256)
-            xs[:, cols] = (xs[:, cols].astype(F32) + dot(ms[...], value_map[:, cols])).astype(BF)
-
-        pl.when(c < CHUNKS - 3)(lambda: middle(c + 3))
-
-        norm_rows(1)
-        for n in range(0, FF, 256):
-            cols = slice(n, n + 256)
-            gate = dot(hs[...], vg[:, cols])
-            up = dot(hs[...], vu[:, cols])
-            hid[:, cols] = (jax.nn.silu(gate) * up).astype(BF)
-        for n in range(0, D, 256):
-            cols = slice(n, n + 256)
-            xs[:, cols] = (xs[:, cols].astype(F32) + dot(hid[...], vd[:, cols])).astype(BF)
-        norm_rows(None)
-        out[c] = dot(hs[...], vh[...]).astype(BF)
+        interleave(attention_steps(both), gates[4:])
+        leave_attention(1 - slot)
+        interleave(down_steps(slot), norm_steps(h2, lambda rows: xb[1 - slot, rows, :], 1))
+        finish(c)
         return 0
 
-    lax.fori_loop(0, CHUNKS, chunk, 0)
+    lax.fori_loop(0, CHUNKS - 1, chunk, 0)
+    interleave(gate_steps())
+    interleave(down_steps((CHUNKS - 1) % 2))
+    finish(CHUNKS - 1)
 
     def drain(c, _):
         copy_sum_a(c).wait_send()
@@ -404,6 +449,9 @@
             vmem((ROWS, D), BF),
             vmem((ROWS, D), BF),
             vmem((ROWS, FF), BF),
+            vmem((2, ROWS, D), BF),
+            vmem((ROWS, D), BF),
+            vmem((ROWS, D), BF),
             vmem((2 * SLOTS, D), BF),
             vmem((2 * SLOTS, D), BF),
             vmem((2 * SLOTS, D), BF),

time: 54.1 us -> 52.9 us (0.978)
  Pallas kernels: 52.2 us -> 51 us
    pallas_call x1, Pallas kernels: 52.2 us -> 51 us  [body(): pl.pallas_call(kernel, out_shape=jax.ShapeDtypeStruct((CHUNKS, ROWS, 2 *...]
where the time goes in v4:
time: 52.9 us; the launch traced here: 52.7 us
  Pallas kernels  51 us (96%)
  local copies, waits for them, and re-layouts  1.67 us (3%)
    pallas_call x1, Pallas kernels, body(): pl.pallas_call(kernel, out_shape=jax.ShapeDtypeStruct((CHUNKS, ROWS, 2 *...  51 us
    unnamed x1, local copies, waits for them, and re-layouts  1.67 us

profile of v4, /device:TPU:1, one launch (start us, length us, event | category | flops | bytes accessed | tf_op | source)
XLA Modules:
  0.0 52.7 jit_solution(4772214263061503897)
XLA Ops:
  0.0 51.0 %fused.1 = bf16[4,256,128]{2,1,0:T(8,128)(2,1)} custom-call(bf16[2,4,2,256,384]{4,3,2,1,0:T(8,128)(2,1)} %spectra.1, bf16[2,8,768,512]{3,2,1,0:T(8,128)(2,1)} %constant.4.clone.tables, bf16[2,512,512]{2,1,0:T(8,128)(2,1)} %constant.5.clone.doppler, bf16[128,1024]{1,0:T(8,128)(2,1)} %w_embed.1, bf16[1,1024,1024]{2,1,0:T(8,128)(2,1)} %w_query.1, ...), custom_call_target="tpu_custom_call" | custom-call | tf_op jit(solution)/shard_map/fused/pallas_call | solution.py:417
  51.0 1.7 %copy.15 = bf16[2,16,32,128]{3,2,1,0:T(8,128)(2,1)} copy(bf16[2,16,32,128]{3,2,1,0:T(8,128)(2,1)} %bitcast.1) | data formatting | bytes 524288

commit v5 on v4

--- a/solution.py
+++ b/solution.py
@@ -191,10 +191,6 @@
         for i in (1, 0, 2):
             copy_sum_b(c, i).start()
 
-    def copy_tile(c, i):
-        target = lax.rem(tm + i, TM)
-        return remote(taps.at[c, target], tiles.at[c, tm], 4, c, {"tm": target})
-
     def all_tiles(c):
         return remote(taps.at[c, pl.ds(0, TM - 1)], tiles.at[c, pl.ds(0, TM - 1)], 4, c, {"tm": other_c})
 
@@ -212,20 +208,26 @@
     pl.semaphore_signal(meet.at[1], inc=1, device_id={"tm": other_c}, device_id_type=MESH)
     pl.semaphore_wait(meet.at[1], 1)
 
+    def send_tiles(c, first):
+        def send(t, _):
+            @pl.when(t != tm)
+            def _():
+                remote(taps.at[c, t], tiles.at[c, tm], 4, c, {"tm": t}).start()
+
+            return 0
+
+        lax.fori_loop(first, first + TM // 2, send, 0)
+
     def reduce(c):
         copy_sum_a(c).wait_recv()
         taps[c, 0:8] = (sum_a[c, mx].astype(F32) + last_a[c].astype(F32)).astype(BF).reshape(TM // 2, 16, 128)
+        send_tiles(c, 0)
         all_sum_b(c).wait_recv()
         total = sum_b[c, my].astype(F32)
         for i in range(YN - 1):
             total = total + last_b[c, i].astype(F32)
         taps[c, 8:16] = total.astype(BF).reshape(TM // 2, 16, 128)
-
-        def send(i, _):
-            copy_tile(c, i).start()
-            return 0
-
-        lax.fori_loop(1, TM, send, 0)
+        send_tiles(c, TM // 2)
         tiles[c, tm] = taps[c, tm]
 
     def parts_left(c):
@@ -384,9 +386,9 @@
 
     def chunk(c, _):
         slot = lax.rem(c, 2)
-        pl.when(c < CHUNKS - 3)(lambda: middle(c + 3))
         gates = gate_steps()
         interleave(gates[:4])
+        pl.when(c < CHUNKS - 3)(lambda: middle(c + 3))
         both = enter(c + 1)
         pl.when(c < CHUNKS - 2)(lambda: reduce(c + 2))
         interleave(attention_steps(both), gates[4:])

time: 52.9 us -> 52.3 us (0.989)
    pallas_call x1, Pallas kernels: 51 us -> 50.5 us  [body(): pl.pallas_call(kernel, out_shape=jax.ShapeDtypeStruct((CHUNKS, ROWS, 2 *...]
where the time goes in v5:
time: 52.3 us; the launch traced here: 52.1 us
  Pallas kernels  50.5 us (97%)
  local copies, waits for them, and re-layouts  1.67 us (3%)
    pallas_call x1, Pallas kernels, body(): pl.pallas_call(kernel, out_shape=jax.ShapeDtypeStruct((CHUNKS, ROWS, 2 *...  50.5 us
    unnamed x1, local copies, waits for them, and re-layouts  1.67 us

profile of v5, /device:TPU:1, one launch (start us, length us, event | category | flops | bytes accessed | tf_op | source)
XLA Modules:
  0.0 52.1 jit_solution(8870352639344973099)
XLA Ops:
  0.0 50.5 %fused.1 = bf16[4,256,128]{2,1,0:T(8,128)(2,1)} custom-call(bf16[2,4,2,256,384]{4,3,2,1,0:T(8,128)(2,1)} %spectra.1, bf16[2,8,768,512]{3,2,1,0:T(8,128)(2,1)} %constant.4.clone.tables, bf16[2,512,512]{2,1,0:T(8,128)(2,1)} %constant.5.clone.doppler, bf16[128,1024]{1,0:T(8,128)(2,1)} %w_embed.1, bf16[1,1024,1024]{2,1,0:T(8,128)(2,1)} %w_query.1, ...), custom_call_target="tpu_custom_call" | custom-call | tf_op jit(solution)/shard_map/fused/pallas_call | solution.py:419
  50.5 1.7 %copy.15 = bf16[2,16,32,128]{3,2,1,0:T(8,128)(2,1)} copy(bf16[2,16,32,128]{3,2,1,0:T(8,128)(2,1)} %bitcast.1) | data formatting | bytes 524288
